TPU v7x, 32 devices: a whole 2x2x4 slice. The times are simulated.
32 devices in a mesh: grp: 2 (over x), tr: 8 (over z, y), ev: 2 (over core).
Axes of the slice: x: 2, y: 2, z: 4, core: 2. Of those that a mesh axis runs over, the one named last changes fastest.
Arguments:
- train_grads: bfloat16 [16384, 1024], P(('grp', 'tr', 'ev')), parts along dimension 0, may hold values from -80 to 80, as said below
- eval_grads: bfloat16 [8192, 1024], P(('grp', 'ev'), 'tr'), parts along dimension 0, may hold values from -6 to 6
- eval_bucket: int32 [8192], P(('grp', 'ev')), parts along dimension 0, may hold values from 0 to 7
- train_valid: int32 [16384], P(('grp', 'tr', 'ev')), parts along dimension 0, may hold values 0 or 1
Outputs:
- scores: bfloat16 [8192, 8192], P(('grp', 'ev'), 'tr'), parts along dimension 0
There are 2 independent parts, one for each index of `grp`. A program takes and returns all parts, laid end to end along the dimension named above; each array names one. Nothing has to cross between parts.
Inputs may be any that keep to these rules, and one draw needn't show every extreme that they name: `train_grads`: real-valued projected gradients.
All inputs are finite; a program needn't handle non-finite values. No bound on the sum of `train_valid` on one device may be relied on, other than what follows from the above.
Results may differ from a plain program's by a relative error of at most 0.012.
Values may be sent and summed in bfloat16 or wider, within the bound.
No kernel may reach another device: no remote copies, remote signals or barrier semaphores. Data moves between devices by JAX's collectives and lax.ppermute only.
A program may use at most 128 MiB of HBM per device.

v0:
```python
import jax
import jax.numpy as jnp
from jax import lax
from jax.sharding import PartitionSpec as P

BUCKETS = 8


damping = 0.1
weight_table = (0.6, 0.9, 1.3, 1.8, 2.4, 3.1, 3.9, 4.8)


def chol_solve(factor, right):
    lower_solved = lax.linalg.triangular_solve(factor, right, left_side=True, lower=True)
    return lax.linalg.triangular_solve(
        factor, lower_solved, left_side=True, lower=True, transpose_a=True
    )


def shards(train_grads, eval_grads, eval_bucket, train_valid):
    rows_here = train_grads.shape[0]
    width = train_grads.shape[1]
    devices_here = lax.axis_size("tr") * lax.axis_size("ev")
    total_rows = rows_here * devices_here
    masked = train_grads * train_valid[:, None].astype(jnp.bfloat16)
    local_gram = jnp.dot(masked.T, train_grads, preferred_element_type=jnp.float32)
    gram_sum = lax.psum(local_gram, ("tr", "ev"))
    hessian = gram_sum / total_rows + damping * jnp.eye(width, dtype=jnp.float32)
    factor = jnp.linalg.cholesky(hessian)
    inverse = chol_solve(factor, jnp.eye(width, dtype=jnp.float32)).astype(jnp.bfloat16)
    precond = jnp.dot(masked, inverse, preferred_element_type=jnp.float32).astype(jnp.bfloat16)
    full_eval = lax.all_gather(eval_grads, "tr", axis=1, tiled=True)
    levels = jnp.arange(BUCKETS, dtype=jnp.int32)
    table_vals = jnp.array(weight_table, dtype=jnp.float32)
    weights = jnp.sum(
        jnp.where(eval_bucket[:, None] == levels[None, :], table_vals[None, :], 0.0), axis=1
    ) / jnp.sqrt(jnp.float32(width))
    return (
        jnp.dot(
            full_eval,
            lax.all_gather(precond, "ev", axis=0, tiled=True).T,
            preferred_element_type=jnp.float32,
        )
        * weights[:, None]
    ).astype(jnp.bfloat16)


def solution(mesh):
    in_specs = (
        P(("grp", "tr", "ev"), None),
        P(("grp", "ev"), "tr"),
        P(("grp", "ev")),
        P(("grp", "tr", "ev")),
    )
    out_specs = P(("grp", "ev"), "tr")
    return jax.shard_map(shards, mesh=mesh, in_specs=in_specs, out_specs=out_specs, check_vma=False)
```

profile of v0, /device:TPU:0, one launch (start us, length us, event | category | flops | bytes accessed | tf_op | source)
XLA Modules:
  0.0 620.0 jit_solution(14695344287071708039)
XLA Ops:
  7.2 4.9 fusion.32
  12.5 2.4 fusion.2
  15.0 111.5 %all-reduce.3.cloned.1.call-done = f32[1024,1024]{0,1:T(8,128)} async-done(((f32[1024,1024]{0,1:T(8,128)}), f32[1024,1024]{0,1:T(8,128)}) %all-reduce.3.cloned.1.call-update) | async-done | bytes 4194320 | tf_op jit(solution)/shard_map/psum | solution.py:27
  126.5 5.1 select_add_fusion
  131.6 5.6 copy.26
  137.2 4.5 fusion
  143.7 11.7 %cholesky.222 = f32[128,128]{1,0:T(8,128)S(1)} custom-call(f32[128,128]{1,0:T(8,128)S(1)} %cholesky.577), custom_call_target="Cholesky" | custom-call | tf_op jit(solution)/shard_map/jit(cholesky)/cholesky | solution.py:29
  155.4 9.8 %custom-call.64 = f32[1,128,128]{1,2,0:T(8,128)S(1)} custom-call(f32[1,128,128]{2,1,0:T(8,128)S(1)} %get-tuple-element.61), custom_call_target="InvertDiagBlocksLowerTriangular" | custom-call | tf_op jit(solution)/shard_map/jit(cholesky)/cholesky | solution.py:29
  168.6 11.7 %cholesky.243 = f32[128,128]{1,0:T(8,128)S(1)} custom-call(f32[128,128]{1,0:T(8,128)S(1)} %cholesky.581), custom_call_target="Cholesky" | custom-call | tf_op jit(solution)/shard_map/jit(cholesky)/cholesky | solution.py:29
  180.9 9.8 %custom-call.65 = f32[1,128,128]{1,2,0:T(8,128)S(1)} custom-call(f32[1,128,128]{2,1,0:T(8,128)S(1)} %get-tuple-element.59), custom_call_target="InvertDiagBlocksLowerTriangular" | custom-call | tf_op jit(solution)/shard_map/jit(cholesky)/cholesky | solution.py:29
  193.8 2.4 convolution_subtract_fusion.11
  196.3 11.7 %cholesky.466 = f32[128,128]{1,0:T(8,128)S(1)} custom-call(f32[128,128]{1,0:T(8,128)S(1)} %cholesky.586), custom_call_target="Cholesky" | custom-call | tf_op jit(solution)/shard_map/jit(cholesky)/cholesky | solution.py:29
  208.7 9.8 %custom-call.66 = f32[1,128,128]{1,2,0:T(8,128)S(1)} custom-call(f32[1,128,128]{2,1,0:T(8,128)S(1)} %get-tuple-element.57), custom_call_target="InvertDiagBlocksLowerTriangular" | custom-call | tf_op jit(solution)/shard_map/jit(cholesky)/cholesky | solution.py:29
  219.8 3.3 convolution_subtract_fusion.12
  223.1 11.7 %cholesky.485 = f32[128,128]{1,0:T(8,128)S(1)} custom-call(f32[128,128]{1,0:T(8,128)S(1)} %cholesky.591), custom_call_target="Cholesky" | custom-call | tf_op jit(solution)/shard_map/jit(cholesky)/cholesky | solution.py:29
  235.6 9.8 %custom-call.67 = f32[1,128,128]{1,2,0:T(8,128)S(1)} custom-call(f32[1,128,128]{2,1,0:T(8,128)S(1)} %get-tuple-element.55), custom_call_target="InvertDiagBlocksLowerTriangular" | custom-call | tf_op jit(solution)/shard_map/jit(cholesky)/cholesky | solution.py:29
  246.6 3.1 convolution_subtract_fusion.13
  249.7 12.1 %cholesky.504 = f32[128,128]{1,0:T(8,128)S(1)} custom-call(f32[128,128]{1,0:T(8,128)S(1)} %cholesky.596), custom_call_target="Cholesky" | custom-call | tf_op jit(solution)/shard_map/jit(cholesky)/cholesky | solution.py:29
  262.6 9.8 %custom-call.68 = f32[1,128,128]{1,2,0:T(8,128)S(1)} custom-call(f32[1,128,128]{2,1,0:T(8,128)S(1)} %get-tuple-element.53), custom_call_target="InvertDiagBlocksLowerTriangular" | custom-call | tf_op jit(solution)/shard_map/jit(cholesky)/cholesky | solution.py:29
  273.5 3.1 convolution_subtract_fusion.14
  276.6 11.7 %cholesky.524 = f32[128,128]{1,0:T(8,128)S(1)} custom-call(f32[128,128]{1,0:T(8,128)S(1)} %cholesky.601), custom_call_target="Cholesky" | custom-call | tf_op jit(solution)/shard_map/jit(cholesky)/cholesky | solution.py:29
  289.1 9.8 %custom-call.69 = f32[1,128,128]{1,2,0:T(8,128)S(1)} custom-call(f32[1,128,128]{2,1,0:T(8,128)S(1)} %get-tuple-element.51), custom_call_target="InvertDiagBlocksLowerTriangular" | custom-call | tf_op jit(solution)/shard_map/jit(cholesky)/cholesky | solution.py:29
  299.9 2.8 convolution_subtract_fusion.15
  302.8 11.7 %cholesky.544 = f32[128,128]{1,0:T(8,128)S(1)} custom-call(f32[128,128]{1,0:T(8,128)S(1)} %cholesky.606), custom_call_target="Cholesky" | custom-call | tf_op jit(solution)/shard_map/jit(cholesky)/cholesky | solution.py:29
  315.3 9.8 %custom-call.70 = f32[1,128,128]{1,2,0:T(8,128)S(1)} custom-call(f32[1,128,128]{2,1,0:T(8,128)S(1)} %get-tuple-element.49), custom_call_target="InvertDiagBlocksLowerTriangular" | custom-call | tf_op jit(solution)/shard_map/jit(cholesky)/cholesky | solution.py:29
  328.1 11.7 %cholesky.562 = f32[128,128]{1,0:T(8,128)S(1)} custom-call(f32[128,128]{1,0:T(8,128)S(1)} %convolution_subtract_fusion.16), custom_call_target="Cholesky" | custom-call | tf_op jit(solution)/shard_map/jit(cholesky)/cholesky | solution.py:29
  350.0 4.9 select_select_fusion
  354.9 23.7 %while.1 = (s32[]{:T(128)}, f32[1024,1024]{0,1:T(8,128)}, s32[8,2]{0,1:T(2,128)S(1)}, f32[8,128,128]{2,1,0:T(8,128)S(1)}, s32[]{:T(128)}) while((s32[]{:T(128)}, f32[1024,1024]{0,1:T(8,128)}, s32[8,2]{0,1:T(2,128)S(1)}, f32[8,128,128]{2,1,0:T(8,128)S(1)}, s32[]{:T(128)}) %tuple.51), condition=%wide.while_cond, body=%wide.while_body.sunk | while | flops 2 | bytes 393321 | solution.py:15
  355.6 2.2 dynamic-slice.7
  358.5 2.2 dynamic-slice.7
  361.5 2.2 dynamic-slice.7
  364.5 2.2 dynamic-slice.7
  367.5 2.2 dynamic-slice.7
  370.5 2.2 dynamic-slice.7
  378.7 79.0 %custom-call.71 = f32[8,128,128]{1,2,0:T(8,128)S(1)} custom-call(f32[8,128,128]{2,1,0:T(8,128)S(1)} %get-tuple-element.12), custom_call_target="InvertDiagBlocksLowerTriangular" | custom-call | tf_op jit(solution)/shard_map/triangular_solve | solution.py:15
  458.2 2.3 convolution_subtract_fusion.9
  461.3 3.3 convolution_subtract_fusion.1
  465.3 2.8 fusion.37
  468.8 3.5 fusion.43
  473.0 4.6 convolution_subtract_fusion.5
  478.3 5.1 convolution_subtract_fusion.3
  484.1 6.3 %convolution_subtract_fusion.8 = f32[128,1024]{0,1:T(8,128)S(1)} fusion(f32[896,1024]{1,0:T(8,128)S(1)} %get-tuple-element.68, f32[1024,1024]{0,1:T(8,128)S(1)} %copy-done.2, f32[1024,1024]{0,1:T(8,128)S(1)} %copy-done.1), kind=kOutput, calls=%fused_computation.56 | convolution fusion | flops 1409417216 | bytes 5177344 | tf_op jit(solution)/shard_map/triangular_solve | solution.py:14
  503.7 2.2 convolution_subtract_fusion.6
  507.1 2.3 convolution_convert_fusion
  510.3 8.8 %all-gather.3.cloned.1.call-done = bf16[1024,1024]{1,0:T(8,128)(2,1)} async-done(((bf16[512,1024]{1,0:T(8,128)(2,1)}), bf16[1024,1024]{1,0:T(8,128)(2,1)}) %all-gather.3.cloned.1.call-update) | async-done | bytes 2097168 | tf_op jit(solution)/shard_map/all_gather | solution.py:41
  519.1 78.5 %all-gather.5.cloned.1.call-done = bf16[2048,1024]{1,0:T(8,128)(2,1)} async-done(((bf16[2048,128]{1,0:T(8,128)(2,1)}), bf16[2048,1024]{1,0:T(8,128)(2,1)}) %all-gather.5.cloned.1.call-update) | async-done | bytes 4194320 | tf_op jit(solution)/shard_map/all_gather | solution.py:32
  597.6 9.3 %fusion.1 = bf16[2048,1024]{0,1:T(8,128)(2,1)} fusion(f32[2048]{0:T(1024)S(1)} %broadcast_multiply_fusion, bf16[1024,1024]{1,0:T(8,128)(2,1)} %all-gather.3.cloned.1.call-done, bf16[2048,1024]{1,0:T(8,128)(2,1)} %all-gather.5.cloned.1.call-done), kind=kOutput, calls=%fused_computation.9 | convolution fusion | flops 4299161600 | bytes 10493952 | tf_op jit(solution)/shard_map/dot_general | solution.py:39
  606.9 6.4 %copy.43 = bf16[2048,1024]{1,0:T(8,128)(2,1)} copy(bf16[2048,1024]{0,1:T(8,128)(2,1)} %fusion.1) | data formatting | bytes 8388608 | tf_op jit(solution)/shard_map/convert_element_type | solution.py:45
  (154 shorter events, 56.7 us)
Async XLA Ops:
  6.5 120.0 %all-reduce.3.cloned.1.call-start = ((), (), s32[]{:S(2)}) async-start(), calls=%async_computation | async-start | bytes 8388608 | tf_op jit(solution)/shard_map/psum | solution.py:27
  12.2 506.9 %all-gather.3.cloned.1.call-start = ((), (), s32[]{:S(2)}) async-start(), calls=%async_computation.1 | async-start | bytes 3145728 | tf_op jit(solution)/shard_map/all_gather | solution.py:41
  141.6 2.0 copy-start.3
  191.9 2.0 copy-start
  457.7 3.6 copy-start.1
  460.6 4.7 copy-start.2
  505.9 1.2 copy-start.6
  507.1 3.0 copy-start.4
  507.1 3.1 copy-start.5
  509.5 88.1 %all-gather.5.cloned.1.call-start = ((), (), s32[]{:S(2)}) async-start(), calls=%async_computation.2 | async-start | bytes 4718592 | tf_op jit(solution)/shard_map/all_gather | solution.py:32
Sparse Core Ops, SparseCore 0:
  12.3 114.1 all-reduce.2
  509.6 9.4 all-gather.2
  521.4 76.1 all-gather.4
where the time goes:
time: 624 us; the launch traced here: 620 us
  other arithmetic  265 us (42%)
  waiting for transfers between devices  200 us (32%)
  matrix products  90.2 us (14%)
  local copies, waits for them, and re-layouts  46.3 us (7%)
  between operations  18.9 us (3%)
    another operation x30, other arithmetic, shards(): factor = jnp.linalg.cholesky(hessian)  168 us
    psum x1, waiting for transfers between devices, shards(): gram_sum = lax.psum(local_gram, ('tr', 'ev'))  112 us
    another operation x4, other arithmetic, chol_solve(): lax.linalg.triangular_solve(factor, lower_solved, left_side=True, lower=T...  83.9 us
    all_gather x1, waiting for transfers between devices, shards(): full_eval = lax.all_gather(eval_grads, 'tr', axis=1, tiled=True)  78.5 us
    another operation x15, matrix products, chol_solve(): lax.linalg.triangular_solve(factor, right, left_side=True, lower=True)  33.3 us
    another operation x14, matrix products, shards(): factor = jnp.linalg.cholesky(hessian)  25.9 us
    another operation x40, local copies, waits for them, and re-layouts  23.5 us
    another operation x15, matrix products, chol_solve(): lax.linalg.triangular_solve(factor, lower_solved, left_side=True, lower=T...  14.5 us
  transfers between devices with their start and end apart: 3, of which 3 were waited for; matrix products, arithmetic and copies ran while one was open for 0% of the time, Pallas kernels for 0%

commit v1 on v0

v1 whole, which is shorter than its diff:
```python
import functools

import jax
import jax.numpy as jnp
from jax import lax
from jax.experimental import pallas as pl
from jax.experimental.pallas import tpu as pltpu
from jax.sharding import PartitionSpec as P

BUCKETS = 8
BLK = 128
MIB = 2**20

damping = 0.1
weight_table = (0.6, 0.9, 1.3, 1.8, 2.4, 3.1, 3.9, 4.8)

VMEM = pl.BlockSpec(memory_space=pltpu.VMEM)
SMEM = pl.BlockSpec(memory_space=pltpu.SMEM)


def split3(x):
    hi = x.astype(jnp.bfloat16)
    rest = x - hi.astype(jnp.float32)
    mid = rest.astype(jnp.bfloat16)
    low = (rest - mid.astype(jnp.float32)).astype(jnp.bfloat16)
    return hi, mid, low


def as_left(x):
    hi, mid, low = split3(x)
    return jnp.concatenate([hi, mid, hi, mid, hi, low], axis=1)


def as_right(x):
    hi, mid, low = split3(x)
    return jnp.concatenate([hi, hi, mid, mid, low, hi], axis=0)


def mm(left, right):
    return jnp.dot(left, right, preferred_element_type=jnp.float32)


def across(x, lane):
    return jnp.broadcast_to(x[:, lane : lane + 1], x.shape)


def down(x, row):
    return jnp.broadcast_to(x[row : row + 1, :], x.shape)


def invert_block(block):
    lanes = lax.broadcasted_iota(jnp.int32, (8, BLK), 1)
    subs = lax.broadcasted_iota(jnp.int32, (8, BLK), 0)
    strips = [block[8 * b : 8 * b + 8, :] for b in range(BLK // 8)]
    for m in range(BLK // 8):
        row = strips[m]
        cols = [across(row, 8 * m + t) for t in range(8)]
        for t in range(8):
            pivot = 1.0 / down(cols[t], t)
            here = subs == t
            own = lanes == 8 * m + t
            lead = jnp.where(own, 1.0, down(row, t)) * pivot
            row = jnp.where(here, lead, jnp.where(own, 0.0, row) - cols[t] * lead)
            for s in range(t + 1, 8):
                lead_s = down(cols[s], t)
                cols[s] = jnp.where(here, lead_s * pivot, cols[s] - (cols[t] * lead_s) * pivot)
        strips[m] = row
        done = (lanes >= 8 * m) & (lanes < 8 * m + 8)
        leads = [down(row, t) for t in range(8)]
        for b in range(BLK // 8):
            if b != m:
                old = strips[b]
                new = jnp.where(done, 0.0, old)
                for t in range(8):
                    new = new - across(old, 8 * m + t) * leads[t]
                strips[b] = new
    return jnp.concatenate(strips, axis=0)


def eliminate(src, dst):
    size = src.shape[0]
    rest = size - BLK
    pivot = invert_block(src[0:BLK, 0:BLK])
    right = src[0:BLK, BLK:size]
    left = src[BLK:size, 0:BLK]
    scaled = mm(as_left(pivot), as_right(right))
    left_parts = as_left(left)
    dst[0:rest, rest:size] = -mm(left_parts, as_right(pivot))
    dst[rest:size, 0:rest] = scaled
    dst[rest:size, rest:size] = pivot
    step = 256
    for at in range(0, rest, step):
        n = min(step, rest - at)
        dst[0:rest, at : at + n] = src[BLK:size, BLK + at : BLK + at + n] - mm(
            left_parts, as_right(scaled[:, at : at + n])
        )


def gram_kernel(masked_ref, gram_ref, turned_ref):
    turned_ref[...] = masked_ref[...].T
    blocks = masked_ref.shape[1] // BLK
    half = blocks // 2
    for i in range(half):
        part = mm(
            turned_ref[i * BLK : (i + 1) * BLK, :],
            masked_ref[:, i * BLK : (i + half + 1) * BLK],
        )
        for j in range(half + 1):
            at = (i * (half + 1) + j) * BLK
            gram_ref[at : at + BLK, :] = part[:, j * BLK : (j + 1) * BLK]


def inverse_kernel(total_rows, ev_ref, own_ref, other_ref, out_ref, one, two):
    size = out_ref.shape[0]
    blocks = size // BLK
    half = blocks // 2
    rows = lax.broadcasted_iota(jnp.int32, (BLK, BLK), 0)
    cols = lax.broadcasted_iota(jnp.int32, (BLK, BLK), 1)
    ridge = jnp.where(rows == cols, jnp.float32(damping), 0.0)
    for i in range(blocks):
        source = own_ref if i < half else other_ref
        for j in range(half + 1):
            at = ((i % half) * (half + 1) + j) * BLK
            c = (i + j) % blocks
            value = source[at : at + BLK, :] / total_rows
            if j == 0:
                value = value + ridge
            one[i * BLK : (i + 1) * BLK, c * BLK : (c + 1) * BLK] = value
            if 0 < j < half:
                one[c * BLK : (c + 1) * BLK, i * BLK : (i + 1) * BLK] = value.T

    @pl.loop(0, blocks // 2)
    def _(_):
        eliminate(one, two)
        eliminate(two, one)

    here = ev_ref[0]
    for i in range(blocks):
        to = lax.rem(i + half * here, blocks) * BLK
        out_ref[pl.ds(pl.multiple_of(to, BLK), BLK), :] = one[i * BLK : (i + 1) * BLK, :].astype(jnp.bfloat16)


def score_kernel(eval_ref, weight_ref, inverse_ref, turned_ref, out_ref, precond):
    @pl.when(pl.program_id(0) == 0)
    def _():
        precond[...] = mm(inverse_ref[...], turned_ref[...]).astype(jnp.bfloat16)

    out_ref[...] = (mm(eval_ref[...], precond[...]) * weight_ref[...]).astype(jnp.bfloat16)


def shards(train_grads, eval_grads, eval_bucket, train_valid):
    rows_here, width = train_grads.shape
    total_rows = rows_here * lax.axis_size("tr") * lax.axis_size("ev")
    here = lax.axis_index("ev")
    swap = [(0, 1), (1, 0)]

    masked = train_grads * train_valid[:, None].astype(jnp.bfloat16)
    other_masked = lax.ppermute(masked, "ev", swap)
    chip = jnp.where(
        here == 0,
        jnp.concatenate([masked, other_masked], axis=0),
        jnp.concatenate(
            [jnp.roll(other_masked, width // 2, axis=1), jnp.roll(masked, width // 2, axis=1)], axis=0
        ),
    )
    chip_rows = 2 * rows_here
    held = (width // BLK // 2) * (width // BLK // 2 + 1) * BLK
    local_gram, turned = pl.pallas_call(
        gram_kernel,
        out_shape=(
            jax.ShapeDtypeStruct((held, BLK), jnp.float32),
            jax.ShapeDtypeStruct((width, chip_rows), jnp.bfloat16),
        ),
        in_specs=[VMEM],
        out_specs=(VMEM, VMEM),
        compiler_params=pltpu.CompilerParams(vmem_limit_bytes=32 * MIB),
        cost_estimate=pl.CostEstimate(flops=2 * chip_rows * held * BLK, bytes_accessed=6 * MIB, transcendentals=0),
        name="gram",
    )(chip)
    own_gram = lax.psum(local_gram, "tr")
    other_gram = lax.ppermute(own_gram, "ev", swap)
    eval_grads, own_gram = lax.optimization_barrier((eval_grads, own_gram))
    full_eval = lax.all_gather(eval_grads, "tr", axis=1, tiled=True)

    inverse = pl.pallas_call(
        functools.partial(inverse_kernel, total_rows),
        out_shape=jax.ShapeDtypeStruct((width, width), jnp.bfloat16),
        in_specs=[SMEM, VMEM, VMEM],
        out_specs=VMEM,
        scratch_shapes=[pltpu.VMEM((width, width), jnp.float32)] * 2,
        compiler_params=pltpu.CompilerParams(vmem_limit_bytes=48 * MIB),
        cost_estimate=pl.CostEstimate(flops=40_000_000_000, bytes_accessed=5 * MIB, transcendentals=0),
        name="inverse",
    )(here.reshape(1), own_gram, other_gram)

    levels = jnp.arange(BUCKETS, dtype=jnp.int32)
    table_vals = jnp.array(weight_table, dtype=jnp.float32)
    weights = jnp.sum(
        jnp.where(eval_bucket[:, None] == levels[None, :], table_vals[None, :], 0.0), axis=1
    ) / jnp.sqrt(jnp.float32(width))
    eval_rows = full_eval.shape[0]
    tile = 256
    return pl.pallas_call(
        score_kernel,
        grid=(eval_rows // tile,),
        out_shape=jax.ShapeDtypeStruct((eval_rows, chip_rows), jnp.bfloat16),
        in_specs=[
            pl.BlockSpec((tile, width), lambda i: (i, 0)),
            pl.BlockSpec((tile, 1), lambda i: (i, 0)),
            pl.BlockSpec((width, width), lambda i: (0, 0)),
            pl.BlockSpec((width, chip_rows), lambda i: (0, 0)),
        ],
        out_specs=pl.BlockSpec((tile, chip_rows), lambda i: (i, 0)),
        scratch_shapes=[pltpu.VMEM((width, chip_rows), jnp.bfloat16)],
        compiler_params=pltpu.CompilerParams(vmem_limit_bytes=40 * MIB),
        cost_estimate=pl.CostEstimate(
            flops=2 * (eval_rows + width) * width * chip_rows, bytes_accessed=12 * MIB, transcendentals=0
        ),
        name="scores",
    )(full_eval, weights[:, None], inverse, turned)


def solution(mesh):
    in_specs = (
        P(("grp", "tr", "ev"), None),
        P(("grp", "ev"), "tr"),
        P(("grp", "ev")),
        P(("grp", "tr", "ev")),
    )
    out_specs = P(("grp", "ev"), "tr")
    return jax.shard_map(shards, mesh=mesh, in_specs=in_specs, out_specs=out_specs, check_vma=False)
```

time: 624 us -> 208 us (0.33)
  other arithmetic: 265 us -> 10.5 us
  matrix products: 90.2 us -> 0 us
  waiting for transfers between devices: 200 us -> 112 us
  Pallas kernels: 0 us -> 61.1 us
  local copies, waits for them, and re-layouts: 46.3 us -> 9.86 us
    another operation x34 -> x0, other arithmetic: 251 us -> none  [the longest x30 168 us: shards(): factor = jnp.linalg.cholesky(hessian)]
    another operation x44 -> x0, matrix products: 73.7 us -> none  [the longest x15 33.3 us: chol_solve(): lax.linalg.triangular_solve(factor, right, left_side=True, lower=True)]
    pallas_call x0 -> x3, Pallas kernels: none -> 61.1 us  [the longest x1 49.8 us: shards(): pl.pallas_call(functools.partial(inverse_kernel, total_rows), out_shape=j...]
    all_gather x1, waiting for transfers between devices: 78.5 us -> 21.8 us  [shards(): full_eval = lax.all_gather(eval_grads, 'tr', axis=1, tiled=True)]
    another operation x69 -> x0, local copies, waits for them, and re-layouts: 29.5 us -> none
    psum x1, waiting for transfers between devices: 112 us -> 85.7 us  [shards(): own_gram = lax.psum(local_gram, 'tr')]
    dot_general x3 -> x0, matrix products: 16.5 us -> none  [the longest x1 9.32 us: shards(): jnp.dot(full_eval, lax.all_gather(precond, 'ev', axis=0, tiled=True).T, p...]
    all_gather x1 -> x0, waiting for transfers between devices: 8.79 us -> none  [shards(): lax.all_gather(precond, 'ev', axis=0, tiled=True)]
  transfers between devices with their start and end apart: 3 -> 4, of which waited for: 3 -> 4; matrix products, arithmetic and copies ran while one was open for 0% -> 0% of each run, Pallas kernels for 0% -> 24%
where the time goes in v1:
time: 208 us
  waiting for transfers between devices  112 us (54%)
  Pallas kernels  61.1 us (29%)
  between operations  13.5 us (6%)
  other arithmetic  10.5 us (5%)
  local copies, waits for them, and re-layouts  9.86 us (5%)
    psum x1, waiting for transfers between devices, shards(): own_gram = lax.psum(local_gram, 'tr')  85.7 us
    pallas_call x1, Pallas kernels, shards(): pl.pallas_call(functools.partial(inverse_kernel, total_rows), out_shape=j...  49.8 us
    all_gather x1, waiting for transfers between devices, shards(): full_eval = lax.all_gather(eval_grads, 'tr', axis=1, tiled=True)  21.8 us
    unnamed x16, local copies, waits for them, and re-layouts  9.34 us
    pallas_call x1, Pallas kernels, shards(): pl.pallas_call(score_kernel, grid=(eval_rows // tile,), out_shape=jax.Sha...  9.07 us
    select_n x1, other arithmetic, shards(): jnp.where(here == 0, jnp.concatenate([masked, other_masked], axis=0), jnp...  8.33 us
  transfers between devices with their start and end apart: 4, of which 4 were waited for; matrix products, arithmetic and copies ran while one was open for 0% of the time, Pallas kernels for 24%

profile of v1, /device:TPU:0, one launch (start us, length us, event | category | flops | bytes accessed | tf_op | source)
XLA Modules:
  0.0 208.2 jit_solution(4932250678436749879)
XLA Ops:
  6.5 0.0 all-reduce.2.cloned.1.call-start
  6.5 0.7 convert_element_type.4
  7.2 1.4 broadcast_multiply_fusion
  8.6 0.5 collective-permute-start
  9.1 0.1 fusion.1
  9.2 2.2 %collective-permute-done = bf16[512,1024]{1,0:T(8,128)(2,1)S(1)} collective-permute-done((bf16[512,1024]{1,0:T(8,128)(2,1)S(1)}, bf16[512,1024]{1,0:T(8,128)(2,1)S(1)}, u32[]{:S(2)}, u32[]{:S(2)}) %collective-permute-start) | collective-permute-done | bytes 1048608 | tf_op jit(solution)/shard_map/ppermute | solution.py:158
  11.4 0.1 fusion
  11.5 8.3 %maximum_select_fusion.masked_ref = bf16[1024,1024]{1,0:T(8,128)(2,1)S(1)} fusion(bf16[512,1024]{1,0:T(8,128)(2,1)S(1)} %collective-permute-done, bf16[512,1024]{1,0:T(8,128)(2,1)S(1)} %broadcast_multiply_fusion, bf16[512,512]{1,0:T(8,128)(2,1)S(1)} %get-tuple-element.16, bf16[512,512]{1,0:T(8,128)(2,1)S(1)} %get-tuple-element.15, ...), kind=kLoop, calls=%fused_computation | loop fusion | flops 13631488 | bytes 6291457 | tf_op jit(solution)/shard_map/jit(_where)/select_n | solution.py:159
  19.8 0.0 copy-start.6
  19.8 0.0 copy-start.7
  19.8 2.2 %gram.1 = (f32[2560,128]{1,0:T(8,128)}, bf16[1024,1024]{1,0:T(8,128)(2,1)S(1)}) custom-call(bf16[1024,1024]{1,0:T(8,128)(2,1)S(1)} %maximum_select_fusion.masked_ref), custom_call_target="tpu_custom_call" | custom-call | flops 671088640 | bytes 6291456 | tf_op jit(solution)/shard_map/gram/pallas_call | solution.py:168
  22.1 0.0 copy-start.2
  22.1 1.3 copy-done.2
  23.4 0.0 all-reduce.2.cloned.1.call-update
  23.4 0.2 all-gather.2.cloned.1.call-start
  23.7 85.7 %all-reduce.2.cloned.1.call-done.own_ref = f32[2560,128]{1,0:T(8,128)} async-done(((f32[2560,128]{1,0:T(8,128)}), f32[2560,128]{1,0:T(8,128)}) %all-reduce.2.cloned.1.call-update) | async-done | bytes 1310736 | tf_op jit(solution)/shard_map/psum | solution.py:180
  109.4 0.0 all-gather.2.cloned.1.call-update
  109.4 0.1 collective-permute-start.1
  109.5 0.0 copy-done.6
  109.5 0.0 copy-done.7
  109.5 0.1 select_reduce_fusion
  109.6 0.4 copy.7.weight_ref
  110.0 2.7 %collective-permute-done.1.other_ref = f32[2560,128]{1,0:T(8,128)S(1)} collective-permute-done((f32[2560,128]{1,0:T(8,128)}, f32[2560,128]{1,0:T(8,128)S(1)}, u32[]{:S(2)}, u32[]{:S(2)}) %collective-permute-start.1) | collective-permute-done | bytes 1310752 | tf_op jit(solution)/shard_map/ppermute | solution.py:181
  112.7 0.0 copy-start.1
  112.7 1.3 copy-done.1
  114.0 49.8 %inverse.1.inverse_ref = bf16[1024,1024]{1,0:T(8,128)(2,1)S(1)} custom-call(s32[1]{0:T(128)} %bitcast.1.ev_ref, f32[2560,128]{1,0:T(8,128)S(1)} %copy-done.1, f32[2560,128]{1,0:T(8,128)S(1)} %collective-permute-done.1.other_ref), custom_call_target="tpu_custom_call" | custom-call | flops 40000000000 | bytes 5242880 | tf_op jit(solution)/shard_map/inverse/pallas_call | solution.py:185
  163.8 0.0 copy-start.4
  163.8 1.3 copy-done.4
  165.1 21.8 %all-gather.2.cloned.1.call-done.eval_ref = bf16[2048,1024]{1,0:T(8,128)(2,1)} async-done(((bf16[2048,128]{1,0:T(8,128)(2,1)}), bf16[2048,1024]{1,0:T(8,128)(2,1)}) %all-gather.2.cloned.1.call-update) | async-done | bytes 4194320 | tf_op jit(solution)/shard_map/all_gather | solution.py:183
  186.9 0.0 copy-start
  186.9 2.2 %copy-done = bf16[2048,1024]{1,0:T(8,128)(2,1)S(1)} copy-done((bf16[2048,1024]{1,0:T(8,128)(2,1)S(1)}, bf16[2048,1024]{1,0:T(8,128)(2,1)}, u32[]{:S(2)}) %copy-start) | copy-done | bytes 4194328
  189.1 0.0 copy-start.3
  189.1 1.6 copy-done.3
  190.7 0.0 copy-start.5
  190.7 1.6 copy-done.5
  192.3 9.1 %scores.1 = bf16[2048,1024]{1,0:T(8,128)(2,1)} custom-call(bf16[2048,1024]{1,0:T(8,128)(2,1)S(1)} %copy-done, f32[2048,1]{1,0:T(8,128)S(1)} %copy.7.weight_ref, bf16[1024,1024]{1,0:T(8,128)(2,1)S(1)} %copy-done.5, bf16[1024,1024]{1,0:T(8,128)(2,1)S(1)} %copy-done.3), custom_call_target="tpu_custom_call" | custom-call | flops 6442450944 | bytes 12582912 | tf_op jit(solution)/shard_map/scores/pallas_call | solution.py:203
  (1 shorter events, 0.0 us)
Async XLA Ops:
  6.5 102.8 %all-reduce.2.cloned.1.call-start = ((), (), s32[]{:S(2)}) async-start(), calls=%async_computation | async-start | bytes 2621440 | tf_op jit(solution)/shard_map/psum | solution.py:180
  8.6 2.8 %collective-permute-start = (bf16[512,1024]{1,0:T(8,128)(2,1)S(1)}, bf16[512,1024]{1,0:T(8,128)(2,1)S(1)}, u32[]{:S(2)}, u32[]{:S(2)}) collective-permute-start(bf16[512,1024]{1,0:T(8,128)(2,1)S(1)} %broadcast_multiply_fusion), channel_id=1, source_target_pairs={{0,1},{1,0},{2,3},{3,2},{4,5},{5,4},{6,7},{7,6},{8,9},{9,8},{10,11... | collective-permute-start | bytes 3145736 | tf_op jit(solution)/shard_map/ppermute | solution.py:158
  19.8 89.7 %copy-start.6 = (s32[2048]{0:T(1024)S(1)}, s32[2048]{0:T(1024)}, u32[]{:S(2)}) copy-start(s32[2048]{0:T(1024)} %param.7) | copy-start | bytes 24580
  19.8 89.7 %copy-start.7 = (f32[8]{0:T(128)S(1)}, f32[8]{0:T(128)}, u32[]{:S(2)}) copy-start(f32[8]{0:T(128)} %constant.13.clone) | copy-start | bytes 100
  22.1 1.3 copy-start.2
  23.4 163.5 %all-gather.2.cloned.1.call-start = ((), (), s32[]{:S(2)}) async-start(), calls=%async_computation.1 | async-start | bytes 4718592 | tf_op jit(solution)/shard_map/all_gather | solution.py:183
  109.4 3.3 %collective-permute-start.1 = (f32[2560,128]{1,0:T(8,128)}, f32[2560,128]{1,0:T(8,128)S(1)}, u32[]{:S(2)}, u32[]{:S(2)}) collective-permute-start(f32[2560,128]{1,0:T(8,128)} %all-reduce.2.cloned.1.call-done.own_ref), channel_id=1, source_target_pairs={{0,1},{1,0},{2,3},{3,2},{4,5},{5,4},{6,7},{7,6},{8,9},{9,8},{10,11... | collective-permute-start | bytes 3932168 | tf_op jit(solution)/shard_map/ppermute | solution.py:181
  112.7 1.3 copy-start.1
  163.8 1.3 copy-start.4
  186.9 2.2 %copy-start = (bf16[2048,1024]{1,0:T(8,128)(2,1)S(1)}, bf16[2048,1024]{1,0:T(8,128)(2,1)}, u32[]{:S(2)}) copy-start(bf16[2048,1024]{1,0:T(8,128)(2,1)} %all-gather.2.cloned.1.call-done.eval_ref) | copy-start | bytes 12582916
  189.1 1.6 copy-start.3
  190.7 1.6 copy-start.5
Sparse Core Ops, SparseCore 0:
  23.6 85.7 all-reduce.1
  111.6 75.2 all-gather.1

commit v2 on v1

v2 whole, which is shorter than its diff:
```python
import functools

import jax
import jax.numpy as jnp
from jax import lax
from jax.experimental import pallas as pl
from jax.experimental.pallas import tpu as pltpu
from jax.sharding import PartitionSpec as P

BUCKETS = 8
BLK = 128
MIB = 2**20

damping = 0.1
weight_table = (0.6, 0.9, 1.3, 1.8, 2.4, 3.1, 3.9, 4.8)

VMEM = pl.BlockSpec(memory_space=pltpu.VMEM)
SMEM = pl.BlockSpec(memory_space=pltpu.SMEM)

def split3(x):
    hi = x.astype(jnp.bfloat16)
    rest = x - hi.astype(jnp.float32)
    mid = rest.astype(jnp.bfloat16)
    low = (rest - mid.astype(jnp.float32)).astype(jnp.bfloat16)
    return hi, mid, low


def as_left(x):
    hi, mid, low = split3(x)
    return jnp.concatenate([hi, mid, hi, mid, hi, low], axis=1)


def as_right(x):
    hi, mid, low = split3(x)
    return jnp.concatenate([hi, hi, mid, mid, low, hi], axis=0)


def mm(left, right):
    return jnp.dot(left, right, preferred_element_type=jnp.float32)


def across(x, lane):
    return jnp.broadcast_to(x[:, lane : lane + 1], x.shape)


def down(x, row):
    return jnp.broadcast_to(x[row : row + 1, :], x.shape)


def total(terms):
    while len(terms) > 1:
        terms = [a + b for a, b in zip(terms[::2], terms[1::2])] + terms[len(terms) & ~1 :]
    return terms[0]


def invert_block(block, beside=()):
    lanes = lax.broadcasted_iota(jnp.int32, (8, BLK), 1)
    subs = lax.broadcasted_iota(jnp.int32, (8, BLK), 0)
    count = BLK // 8
    strips = [block[8 * b : 8 * b + 8, :] for b in range(count)]
    for m in range(count):
        row = strips[m]
        cols = [across(row, 8 * m + t) for t in range(8)]
        for t in range(0, 8, 2):
            first, second = cols[t], cols[t + 1]
            a, b, c = down(first, t), down(second, t), down(second, t + 1)
            scale = 1.0 / (a * c - b * b)
            at_first, at_second = subs == t, subs == t + 1
            own_first, own_second = lanes == 8 * m + t, lanes == 8 * m + t + 1
            upper = jnp.where(own_first, 1.0, jnp.where(own_second, 0.0, down(row, t)))
            lower = jnp.where(own_second, 1.0, jnp.where(own_first, 0.0, down(row, t + 1)))
            lead_first = c * upper - b * lower
            lead_second = a * lower - b * upper
            swept = first * lead_first + second * lead_second
            rest = jnp.where(own_first | own_second, 0.0, row) - swept * scale
            row = jnp.where(at_first, lead_first * scale, jnp.where(at_second, lead_second * scale, rest))
            for s in range(t + 2, 8):
                upper, lower = down(cols[s], t), down(cols[s], t + 1)
                lead_first = c * upper - b * lower
                lead_second = a * lower - b * upper
                swept = first * lead_first + second * lead_second
                cols[s] = jnp.where(
                    at_first,
                    lead_first * scale,
                    jnp.where(at_second, lead_second * scale, cols[s] - swept * scale),
                )
        strips[m] = row
        done = (lanes >= 8 * m) & (lanes < 8 * m + 8)
        leads = [down(row, t) for t in range(8)]
        for b in [*range(m + 1, count), *range(m)]:
            old = strips[b]
            strips[b] = jnp.where(done, 0.0, old) - total([across(old, 8 * m + t) * leads[t] for t in range(8)])
        if m < len(beside):
            beside[m]()
    return jnp.concatenate(strips, axis=0)


def eliminate(src, dst, held, left_ref, right_ref, last=False):
    size = src.shape[0]
    rest = size - BLK
    pivot = held[...]
    scaled = mm(as_left(pivot), as_right(src[0:BLK, BLK:size]))
    left_ref[...] = as_left(src[BLK:size, 0:BLK])
    right_ref[...] = as_right(scaled)
    dst[rest:size, 0:rest] = scaled
    dst[rest:size, rest:size] = pivot

    def strip(top, tall, at, wide):
        def run():
            dst[top : top + tall, at : at + wide] = src[
                BLK + top : BLK + top + tall, BLK + at : BLK + at + wide
            ] - mm(left_ref[top : top + tall, :], right_ref[:, at : at + wide])

        return run

    def border():
        dst[0:rest, rest:size] = -mm(left_ref[...], as_right(pivot))

    wide = 2 * BLK
    work = [strip(0, rest, at, min(wide, rest - at)) for at in range(0, rest, wide)] + [border]
    if last:
        for piece in work:
            piece()
    else:
        ahead = src[BLK : 2 * BLK, BLK : 2 * BLK] - mm(left_ref[0:BLK, :], right_ref[:, 0:BLK])
        spread = []
        for piece in work:
            spread += [piece, lambda: None]
        held[...] = invert_block(ahead, spread)


def gram_kernel(ev_ref, own_ref, other_ref, valid_ref, *refs):
    parts, turned_ref, chip = refs[:-2], refs[-2], refs[-1]
    here = ev_ref[0]
    rows, width = own_ref.shape
    blocks = width // BLK
    half = blocks // 2
    middle = width // 2
    for order, ref in ((here, own_ref), (1 - here, other_ref)):
        at = pl.ds(pl.multiple_of(order * rows, rows), rows)
        for side in range(2):
            to = pl.ds(pl.multiple_of((here + side) % 2 * middle, middle), middle)
            piece = ref[:, side * middle : (side + 1) * middle]
            chip[at, to] = piece
            turned_ref[to, at] = piece.T
    turned_ref[...] = turned_ref[...] * valid_ref[...].astype(jnp.float32).astype(jnp.bfloat16)
    each = half * (half + 1) // len(parts)
    for i in range(half):
        part = mm(
            turned_ref[i * BLK : (i + 1) * BLK, :],
            chip[:, i * BLK : (i + half + 1) * BLK],
        )
        for j in range(half + 1):
            n = i * (half + 1) + j
            at = n % each * BLK
            parts[n // each][at : at + BLK, :] = part[:, j * BLK : (j + 1) * BLK]


def inverse_kernel(total_rows, ev_ref, *refs):
    *parts, out_ref, one, two, held, left_ref, right_ref = refs
    size = out_ref.shape[0]
    blocks = size // BLK
    half = blocks // 2
    each = parts[0].shape[0] // BLK
    rows = lax.broadcasted_iota(jnp.int32, (BLK, BLK), 0)
    cols = lax.broadcasted_iota(jnp.int32, (BLK, BLK), 1)
    ridge = jnp.where(rows == cols, jnp.float32(damping), 0.0)
    for i in range(blocks):
        for j in range(half + 1):
            n = i * (half + 1) + j
            at = n % each * BLK
            c = (i + j) % blocks
            value = parts[n // each][at : at + BLK, :] / total_rows
            if j == 0:
                value = value + ridge
            one[i * BLK : (i + 1) * BLK, c * BLK : (c + 1) * BLK] = value
            if 0 < j < half:
                one[c * BLK : (c + 1) * BLK, i * BLK : (i + 1) * BLK] = value.T

    held[...] = invert_block(one[0:BLK, 0:BLK])

    @pl.loop(0, blocks // 2 - 1)
    def _(_):
        eliminate(one, two, held, left_ref, right_ref)
        eliminate(two, one, held, left_ref, right_ref)

    eliminate(one, two, held, left_ref, right_ref)
    eliminate(two, one, held, left_ref, right_ref, last=True)
    here = ev_ref[0]
    for i in range(blocks):
        to = lax.rem(i + half * here, blocks) * BLK
        out_ref[pl.ds(pl.multiple_of(to, BLK), BLK), :] = one[i * BLK : (i + 1) * BLK, :].astype(jnp.bfloat16)


def score_kernel(eval_ref, weight_ref, inverse_ref, turned_ref, out_ref, precond):
    @pl.when(pl.program_id(0) == 0)
    def _():
        precond[...] = mm(inverse_ref[...], turned_ref[...]).astype(jnp.bfloat16)

    out_ref[...] = (mm(eval_ref[...], precond[...]) * weight_ref[...]).astype(jnp.bfloat16)


def shift(members, stride, by):
    n = lax.axis_size("tr")
    pairs = []
    for i in range(n):
        p = i // stride % members
        pairs.append((i, i + ((p + by) % members - p) * stride))
    return pairs


def scatter_sum(x, members, stride):
    me = lax.axis_index("tr") // stride % members
    chunks = x.reshape(members, -1, BLK)
    mine = lax.dynamic_index_in_dim(chunks, me, keepdims=False)
    got = [
        lax.ppermute(
            lax.dynamic_index_in_dim(chunks, (me + by) % members, keepdims=False), "tr", shift(members, stride, by)
        )
        for by in range(1, members)
    ]
    for piece in got:
        mine = mine + piece
    return mine


def collect(x, members, stride):
    me = lax.axis_index("tr") // stride % members
    got = [x] + [lax.ppermute(x, "tr", shift(members, stride, by)) for by in range(members - 1, 0, -1)]
    if members == 2:
        whole = jnp.where(
            me == 0, jnp.concatenate(got, axis=0), jnp.concatenate(got[::-1], axis=0)
        )
        return whole
    twice = jnp.concatenate(got + got, axis=0)
    return lax.dynamic_slice_in_dim(twice, (members - me) * x.shape[0], members * x.shape[0])


def sum_over_tr(parts):
    n = lax.axis_size("tr")
    inner = 2 ** ((n.bit_length() - 1) // 2)
    axes = [(inner, 1), (n // inner, inner)]
    orders = [axes, axes[::-1]]
    parts = [scatter_sum(x, *order[0]) for x, order in zip(parts, orders)]
    parts = [scatter_sum(x, *order[1]) for x, order in zip(parts, orders)]
    parts = [collect(x, *order[1]) for x, order in zip(parts, orders)]
    return [collect(x, *order[0]) for x, order in zip(parts, orders)]


def shards(train_grads, eval_grads, eval_bucket, train_valid):
    rows_here, width = train_grads.shape
    total_rows = rows_here * lax.axis_size("tr") * lax.axis_size("ev")
    here = lax.axis_index("ev")
    swap = [(0, 1), (1, 0)]
    full_eval = lax.all_gather(eval_grads, "tr", axis=1, tiled=True)

    other_train = lax.ppermute(train_grads, "ev", swap)
    other_valid = lax.ppermute(train_valid, "ev", swap)
    chip_valid = jnp.where(
        here == 0, jnp.concatenate([train_valid, other_valid]), jnp.concatenate([other_valid, train_valid])
    )
    chip_rows = 2 * rows_here
    half = width // BLK // 2
    held = half * (half + 1) * BLK
    *local_gram, turned = pl.pallas_call(
        gram_kernel,
        out_shape=(
            *[jax.ShapeDtypeStruct((held // 2, BLK), jnp.float32)] * 2,
            jax.ShapeDtypeStruct((width, chip_rows), jnp.bfloat16),
        ),
        in_specs=[SMEM, VMEM, VMEM, VMEM],
        out_specs=(VMEM,) * 3,
        scratch_shapes=[pltpu.VMEM((chip_rows, width), jnp.bfloat16)],
        compiler_params=pltpu.CompilerParams(vmem_limit_bytes=56 * MIB),
        cost_estimate=pl.CostEstimate(flops=2 * chip_rows * held * BLK, bytes_accessed=6 * MIB, transcendentals=0),
        name="gram",
    )(here.reshape(1), train_grads, other_train, chip_valid[None, :])
    own_gram = sum_over_tr(local_gram)
    other_gram = [lax.ppermute(x, "ev", swap) for x in own_gram]

    inverse = pl.pallas_call(
        functools.partial(inverse_kernel, total_rows),
        out_shape=jax.ShapeDtypeStruct((width, width), jnp.bfloat16),
        in_specs=[SMEM] + [VMEM] * 4,
        out_specs=VMEM,
        scratch_shapes=[
            pltpu.VMEM((width, width), jnp.float32),
            pltpu.VMEM((width, width), jnp.float32),
            pltpu.VMEM((BLK, BLK), jnp.float32),
            pltpu.VMEM((width - BLK, 6 * BLK), jnp.bfloat16),
            pltpu.VMEM((6 * BLK, width - BLK), jnp.bfloat16),
        ],
        compiler_params=pltpu.CompilerParams(vmem_limit_bytes=56 * MIB),
        cost_estimate=pl.CostEstimate(flops=30_000_000_000, bytes_accessed=5 * MIB, transcendentals=0),
        name="inverse",
    )(here.reshape(1), *own_gram, *other_gram)

    levels = jnp.arange(BUCKETS, dtype=jnp.int32)
    table_vals = jnp.array(weight_table, dtype=jnp.float32)
    weights = jnp.sum(
        jnp.where(eval_bucket[:, None] == levels[None, :], table_vals[None, :], 0.0), axis=1
    ) / jnp.sqrt(jnp.float32(width))
    eval_rows = full_eval.shape[0]
    tile = 256
    return pl.pallas_call(
        score_kernel,
        grid=(eval_rows // tile,),
        out_shape=jax.ShapeDtypeStruct((eval_rows, chip_rows), jnp.bfloat16),
        in_specs=[
            pl.BlockSpec((tile, width), lambda i: (i, 0)),
            pl.BlockSpec((tile, 1), lambda i: (i, 0)),
            pl.BlockSpec((width, width), lambda i: (0, 0)),
            pl.BlockSpec((width, chip_rows), lambda i: (0, 0)),
        ],
        out_specs=pl.BlockSpec((tile, chip_rows), lambda i: (i, 0)),
        scratch_shapes=[pltpu.VMEM((width, chip_rows), jnp.bfloat16)],
        compiler_params=pltpu.CompilerParams(vmem_limit_bytes=56 * MIB),
        cost_estimate=pl.CostEstimate(
            flops=2 * (eval_rows + width) * width * chip_rows, bytes_accessed=12 * MIB, transcendentals=0
        ),
        name="scores",
    )(full_eval, weights[:, None], inverse, turned)


def solution(mesh):
    in_specs = (
        P(("grp", "tr", "ev"), None),
        P(("grp", "ev"), "tr"),
        P(("grp", "ev")),
        P(("grp", "tr", "ev")),
    )
    out_specs = P(("grp", "ev"), "tr")
    return jax.shard_map(shards, mesh=mesh, in_specs=in_specs, out_specs=out_specs, check_vma=False)
```

time: 208 us -> 200 us (0.962)
  waiting for transfers between devices: 112 us -> 87.1 us
  starting transfers between devices: 0.81 us -> 25 us
  other arithmetic: 10.5 us -> 2.54 us
  Pallas kernels: 61.1 us -> 65.1 us
  local copies, waits for them, and re-layouts: 9.86 us -> 5.96 us
    psum x1 -> x0, waiting for transfers between devices: 85.7 us -> none  [shards(): own_gram = lax.psum(local_gram, 'tr')]
    ppermute x2 -> x20, waiting for transfers between devices: 4.94 us -> 86.8 us  [the longest x8 46.1 us: scatter_sum(): lax.ppermute(lax.dynamic_index_in_dim(chunks, (me + by) % members, keepdi...]
    ppermute x2 -> x20, starting transfers between devices: 0.59 us -> 25 us  [the longest x8 13.2 us: scatter_sum(): lax.ppermute(lax.dynamic_index_in_dim(chunks, (me + by) % members, keepdi...]
    all_gather x1, waiting for transfers between devices: 21.8 us -> 0.01 us  [shards(): full_eval = lax.all_gather(eval_grads, 'tr', axis=1, tiled=True)]
    unnamed x16 -> x28, local copies, waits for them, and re-layouts: 9.34 us -> 2.24 us
    select_n x1 -> x2, other arithmetic: 8.33 us -> 1.4 us  [the longest x1 1.36 us: shards(): jnp.where(here == 0, jnp.concatenate([train_valid, other_valid]), jnp.con...]
    pallas_call x1, Pallas kernels: 9.07 us -> 13.1 us  [shards(): pl.pallas_call(score_kernel, grid=(eval_rows // tile,), out_shape=jax.Sha...]
    pallas_call x1, Pallas kernels: 2.24 us -> 5.03 us  [shards(): pl.pallas_call(gram_kernel, out_shape=(*[jax.ShapeDtypeStruct((held // 2,...]
  transfers between devices with their start and end apart: 4 -> 21, of which waited for: 4 -> 12; matrix products, arithmetic and copies ran while one was open for 0% -> 3% of each run, Pallas kernels for 24% -> 26%
where the time goes in v2:
time: 200 us; the launch traced here: 199 us
  waiting for transfers between devices  87.1 us (44%)
  Pallas kernels  65.1 us (33%)
  starting transfers between devices  25 us (12%)
  between operations  13.7 us (7%)
  local copies, waits for them, and re-layouts  5.96 us (3%)
  other arithmetic  2.54 us (1%)
    pallas_call x1, Pallas kernels, shards(): pl.pallas_call(functools.partial(inverse_kernel, total_rows), out_shape=j...  47 us
    ppermute x8, waiting for transfers between devices, scatter_sum(): lax.ppermute(lax.dynamic_index_in_dim(chunks, (me + by) % members, keepdi...  46.1 us
    ppermute x8, waiting for transfers between devices, collect(): lax.ppermute(x, 'tr', shift(members, stride, by))  38.5 us
    ppermute x8, starting transfers between devices, scatter_sum(): lax.ppermute(lax.dynamic_index_in_dim(chunks, (me + by) % members, keepdi...  13.2 us
    pallas_call x1, Pallas kernels, shards(): pl.pallas_call(score_kernel, grid=(eval_rows // tile,), out_shape=jax.Sha...  13.1 us
    ppermute x8, starting transfers between devices, collect(): lax.ppermute(x, 'tr', shift(members, stride, by))  10.7 us
    pallas_call x1, Pallas kernels, shards(): pl.pallas_call(gram_kernel, out_shape=(*[jax.ShapeDtypeStruct((held // 2,...  5.03 us
  transfers between devices with their start and end apart: 21, of which 12 were waited for; matrix products, arithmetic and copies ran while one was open for 3% of the time, Pallas kernels for 26%

profile of v2, /device:TPU:0, one launch (start us, length us, event | category | flops | bytes accessed | tf_op | source)
XLA Modules:
  0.0 199.4 jit_solution(12810343338358762782)
XLA Ops:
  6.5 0.5 collective-permute-start
  7.0 0.3 all-gather.2.cloned.1.call-update
  7.3 0.5 collective-permute-start.1
  7.8 1.7 collective-permute-done.1
  9.5 1.4 broadcast_select_fusion.valid_ref
  10.9 1.0 copy-done.5
  11.8 5.0 %gram.1 = (f32[1280,128]{1,0:T(8,128)}, f32[1280,128]{1,0:T(8,128)}, bf16[1024,1024]{1,0:T(8,128)(2,1)}) custom-call(s32[1]{0:T(128)} %bitcast.1.ev_ref, bf16[512,1024]{1,0:T(8,128)(2,1)} %own_ref.1, bf16[512,1024]{1,0:T(8,128)(2,1)} %copy-done.5, s32[1,1024]{1,0:T(1,128)} %broadcast_select_fusion.valid_ref), custom_call_target="tpu_custom_call" | custom-call | flops 671088640 | bytes 6291456 | tf_op jit(solution)/shard_map/gram/pallas_call | solution.py:265
  16.9 1.2 dynamic-slice_bitcast_fusion.3
  18.0 3.0 %collective-permute-start.10 = (f32[320,128]{1,0:T(8,128)S(1)}, f32[320,128]{1,0:T(8,128)S(1)}, u32[]{:S(2)}, u32[]{:S(2)}) collective-permute-start(f32[320,128]{1,0:T(8,128)S(1)} %get-tuple-element.15), channel_id=1, source_target_pairs={{0,4},{2,6},{4,8},{6,10},{8,12},{10,14},{12,0},{14,2},{1,5},{3,7},... | collective-permute-start | bytes 491528 | tf_op jit(solution)/shard_map/ppermute | solution.py:217
  21.1 2.1 %collective-permute-start.12 = (f32[320,128]{1,0:T(8,128)S(1)}, f32[320,128]{1,0:T(8,128)S(1)}, u32[]{:S(2)}, u32[]{:S(2)}) collective-permute-start(f32[320,128]{1,0:T(8,128)S(1)} %get-tuple-element.16), channel_id=1, source_target_pairs={{0,12},{2,14},{4,0},{6,2},{8,4},{10,6},{12,8},{14,10},{1,13},{3,15... | collective-permute-start | bytes 491528 | tf_op jit(solution)/shard_map/ppermute | solution.py:217
  23.2 0.9 collective-permute-start.11
  24.1 1.0 dynamic-slice_bitcast_fusion
  25.1 1.6 collective-permute-start.2
  26.7 4.5 %collective-permute-done.10 = f32[320,128]{1,0:T(8,128)S(1)} collective-permute-done((f32[320,128]{1,0:T(8,128)S(1)}, f32[320,128]{1,0:T(8,128)S(1)}, u32[]{:S(2)}, u32[]{:S(2)}) %collective-permute-start.10) | collective-permute-done | bytes 163872 | tf_op jit(solution)/shard_map/ppermute | solution.py:217
  31.2 5.8 %collective-permute-done.12 = f32[320,128]{1,0:T(8,128)S(1)} collective-permute-done((f32[320,128]{1,0:T(8,128)S(1)}, f32[320,128]{1,0:T(8,128)S(1)}, u32[]{:S(2)}, u32[]{:S(2)}) %collective-permute-start.12) | collective-permute-done | bytes 163872 | tf_op jit(solution)/shard_map/ppermute | solution.py:217
  37.0 15.7 %collective-permute-done.11 = f32[320,128]{1,0:T(8,128)S(1)} collective-permute-done((f32[320,128]{1,0:T(8,128)S(1)}, f32[320,128]{1,0:T(8,128)S(1)}, u32[]{:S(2)}, u32[]{:S(2)}) %collective-permute-start.11) | collective-permute-done | bytes 163872 | tf_op jit(solution)/shard_map/ppermute | solution.py:217
  52.7 1.0 fusion.1
  53.7 1.7 collective-permute-start.13
  55.4 3.0 %collective-permute-done.13 = f32[160,128]{1,0:T(8,128)S(1)} collective-permute-done((f32[160,128]{1,0:T(8,128)S(1)}, f32[160,128]{1,0:T(8,128)S(1)}, u32[]{:S(2)}, u32[]{:S(2)}) %collective-permute-start.13) | collective-permute-done | bytes 81952 | tf_op jit(solution)/shard_map/ppermute | solution.py:217
  58.4 1.7 collective-permute-start.14
  60.1 0.1 collective-permute-start.3
  60.2 3.8 %collective-permute-start.5 = (f32[160,128]{1,0:T(8,128)S(1)}, f32[160,128]{1,0:T(8,128)S(1)}, u32[]{:S(2)}, u32[]{:S(2)}) collective-permute-start(f32[160,128]{1,0:T(8,128)S(1)} %get-tuple-element.19), channel_id=1, source_target_pairs={{0,12},{2,14},{4,0},{6,2},{8,4},{10,6},{12,8},{14,10},{1,13},{3,15... | collective-permute-start | bytes 245768 | tf_op jit(solution)/shard_map/ppermute | solution.py:217
  64.0 0.6 collective-permute-start.17
  64.6 2.4 %collective-permute-start.16 = (f32[320,128]{1,0:T(8,128)S(1)}, f32[320,128]{1,0:T(8,128)S(1)}, u32[]{:S(2)}, u32[]{:S(2)}) collective-permute-start(f32[320,128]{1,0:T(8,128)S(1)} %get-tuple-element.12), channel_id=1, source_target_pairs={{0,8},{2,10},{4,12},{6,14},{8,0},{10,2},{12,4},{14,6},{1,9},{3,11}... | collective-permute-start | bytes 491528 | tf_op jit(solution)/shard_map/ppermute | solution.py:229
  67.1 1.3 collective-permute-done.3
  68.4 1.5 collective-permute-start.15
  69.9 15.7 %collective-permute-done.4 = f32[160,128]{1,0:T(8,128)S(1)} collective-permute-done((f32[160,128]{1,0:T(8,128)S(1)}, f32[160,128]{1,0:T(8,128)S(1)}, u32[]{:S(2)}, u32[]{:S(2)}) %collective-permute-start.4) | collective-permute-done | bytes 81952 | tf_op jit(solution)/shard_map/ppermute | solution.py:217
  85.7 0.1 collective-permute-start.8
  85.7 0.1 collective-permute-start.7
  85.8 7.3 %collective-permute-done.15 = f32[320,128]{1,0:T(8,128)S(1)} collective-permute-done((f32[320,128]{1,0:T(8,128)S(1)}, f32[320,128]{1,0:T(8,128)S(1)}, u32[]{:S(2)}, u32[]{:S(2)}) %collective-permute-start.15) | collective-permute-done | bytes 163872 | tf_op jit(solution)/shard_map/ppermute | solution.py:229
  93.1 4.3 %collective-permute-start.6 = (f32[160,128]{1,0:T(8,128)S(1)}, f32[160,128]{1,0:T(8,128)S(1)}, u32[]{:S(2)}, u32[]{:S(2)}) collective-permute-start(f32[160,128]{1,0:T(8,128)S(1)} %get-tuple-element.14), channel_id=1, source_target_pairs={{0,12},{2,14},{4,0},{6,2},{8,4},{10,6},{12,8},{14,10},{1,13},{3,15... | collective-permute-start | bytes 245768 | tf_op jit(solution)/shard_map/ppermute | solution.py:229
  97.4 5.4 %collective-permute-done.16 = f32[320,128]{1,0:T(8,128)S(1)} collective-permute-done((f32[320,128]{1,0:T(8,128)S(1)}, f32[320,128]{1,0:T(8,128)S(1)}, u32[]{:S(2)}, u32[]{:S(2)}) %collective-permute-start.16) | collective-permute-done | bytes 163872 | tf_op jit(solution)/shard_map/ppermute | solution.py:229
  102.9 18.0 %collective-permute-done.6 = f32[160,128]{1,0:T(8,128)S(1)} collective-permute-done((f32[160,128]{1,0:T(8,128)S(1)}, f32[160,128]{1,0:T(8,128)S(1)}, u32[]{:S(2)}, u32[]{:S(2)}) %collective-permute-start.6) | collective-permute-done | bytes 81952 | tf_op jit(solution)/shard_map/ppermute | solution.py:229
  121.0 0.1 collective-permute-start.9
  121.1 0.0 copy-start.3
  121.1 0.0 copy-start.4
  121.1 0.1 constant_dynamic-slice_fusion.refs_1_
  121.2 0.1 collective-permute-start.19
  121.3 7.9 %collective-permute-done.9 = f32[640,128]{1,0:T(8,128)S(1)} collective-permute-done((f32[640,128]{1,0:T(8,128)S(1)}, f32[640,128]{1,0:T(8,128)S(1)}, u32[]{:S(2)}, u32[]{:S(2)}) %collective-permute-start.9) | collective-permute-done | bytes 327712 | tf_op jit(solution)/shard_map/ppermute | solution.py:229
  129.2 0.0 copy-start.2
  129.2 0.1 collective-permute-start.18
  129.3 0.1 select_reduce_fusion
  129.4 1.4 copy.7.weight_ref
  130.8 0.6 collective-permute-done.18.refs_2_
  131.4 0.3 copy-done.6
  131.6 0.8 copy-done.7
  132.5 47.0 %inverse.1.inverse_ref = bf16[1024,1024]{1,0:T(8,128)(2,1)} custom-call(s32[1]{0:T(128)} %bitcast.1.ev_ref, f32[1280,128]{1,0:T(8,128)} %copy-done.2, f32[1280,128]{1,0:T(8,128)} %copy-done.1, f32[1280,128]{1,0:T(8,128)} %copy-done.7, f32[1280,128]{1,0:T(8,128)} %copy-done.6), custom_call_target="tpu_custom_call" | custom-call | flops 30000001024 | bytes 5242880 | tf_op jit(solution)/shard_map/inverse/pallas_call | solution.py:281
  179.5 13.1 %scores.1 = bf16[2048,1024]{1,0:T(8,128)(2,1)} custom-call(bf16[2048,1024]{1,0:T(8,128)(2,1)} %all-gather.2.cloned.1.call-done.eval_ref, f32[2048,1]{1,0:T(8,128)} %copy.7.weight_ref, bf16[1024,1024]{1,0:T(8,128)(2,1)} %inverse.1.inverse_ref, bf16[1024,1024]{1,0:T(8,128)(2,1)} %get-tuple-element.10.turned_ref), custom_call_target="tpu_custom_call" | custom-call | flops 6442450944 | bytes 12582912 | tf_op jit(solution)/shard_map/scores/pallas_call | solution.py:305
  (44 shorter events, 0.4 us)
Async XLA Ops:
  6.5 172.9 %all-gather.2.cloned.1.call-start = ((), (), s32[]{:S(2)}) async-start(), calls=%async_computation | async-start | bytes 4718592 | tf_op jit(solution)/shard_map/all_gather | solution.py:255
  6.5 4.3 %collective-permute-start = (bf16[512,1024]{1,0:T(8,128)(2,1)}, bf16[512,1024]{1,0:T(8,128)(2,1)S(1)}, u32[]{:S(2)}, u32[]{:S(2)}) collective-permute-start(bf16[512,1024]{1,0:T(8,128)(2,1)} %own_ref.1), channel_id=1, source_target_pairs={{0,1},{1,0},{2,3},{3,2},{4,5},{5,4},{6,7},{7,6},{8,9},{9,8},{10,11... | collective-permute-start | bytes 3145736 | tf_op jit(solution)/shard_map/ppermute | solution.py:257
  7.3 2.2 %collective-permute-start.1 = (s32[512]{0:T(512)}, s32[512]{0:T(512)S(1)}, u32[]{:S(2)}, u32[]{:S(2)}) collective-permute-start(s32[512]{0:T(512)} %param.8), channel_id=1, source_target_pairs={{0,1},{1,0},{2,3},{3,2},{4,5},{5,4},{6,7},{7,6},{8,9},{9,8},{10,11... | collective-permute-start | bytes 6152 | tf_op jit(solution)/shard_map/ppermute | solution.py:258
  10.9 1.0 copy-start.5
  16.9 43.2 %copy-start = (f32[1280,128]{1,0:T(8,128)S(1)}, f32[1280,128]{1,0:T(8,128)}, u32[]{:S(2)}) copy-start(f32[1280,128]{1,0:T(8,128)} %get-tuple-element.8) | copy-start | bytes 1966084
  18.0 13.2 %collective-permute-start.10 = (f32[320,128]{1,0:T(8,128)S(1)}, f32[320,128]{1,0:T(8,128)S(1)}, u32[]{:S(2)}, u32[]{:S(2)}) collective-permute-start(f32[320,128]{1,0:T(8,128)S(1)} %get-tuple-element.15), channel_id=1, source_target_pairs={{0,4},{2,6},{4,8},{6,10},{8,12},{10,14},{12,0},{14,2},{1,5},{3,7},... | collective-permute-start | bytes 491528 | tf_op jit(solution)/shard_map/ppermute | solution.py:217
  21.1 16.0 %collective-permute-start.12 = (f32[320,128]{1,0:T(8,128)S(1)}, f32[320,128]{1,0:T(8,128)S(1)}, u32[]{:S(2)}, u32[]{:S(2)}) collective-permute-start(f32[320,128]{1,0:T(8,128)S(1)} %get-tuple-element.16), channel_id=1, source_target_pairs={{0,12},{2,14},{4,0},{6,2},{8,4},{10,6},{12,8},{14,10},{1,13},{3,15... | collective-permute-start | bytes 491528 | tf_op jit(solution)/shard_map/ppermute | solution.py:217
  23.2 29.6 %collective-permute-start.11 = (f32[320,128]{1,0:T(8,128)S(1)}, f32[320,128]{1,0:T(8,128)S(1)}, u32[]{:S(2)}, u32[]{:S(2)}) collective-permute-start(f32[320,128]{1,0:T(8,128)S(1)} %get-tuple-element.17), channel_id=1, source_target_pairs={{0,8},{2,10},{4,12},{6,14},{8,0},{10,2},{12,4},{14,6},{1,9},{3,11}... | collective-permute-start | bytes 491528 | tf_op jit(solution)/shard_map/ppermute | solution.py:217
  25.1 34.9 %collective-permute-start.2 = (f32[640,128]{1,0:T(8,128)S(1)}, f32[640,128]{1,0:T(8,128)S(1)}, u32[]{:S(2)}, u32[]{:S(2)}) collective-permute-start(f32[640,128]{1,0:T(8,128)S(1)} %dynamic-slice_bitcast_fusion), channel_id=1, source_target_pairs={{0,2},{2,0},{4,6},{6,4},{8,10},{10,8},{12,14},{14,12},{1,3},{3,1},... | collective-permute-start | bytes 983048 | tf_op jit(solution)/shard_map/ppermute | solution.py:217
  53.7 4.6 %collective-permute-start.13 = (f32[160,128]{1,0:T(8,128)S(1)}, f32[160,128]{1,0:T(8,128)S(1)}, u32[]{:S(2)}, u32[]{:S(2)}) collective-permute-start(f32[160,128]{1,0:T(8,128)S(1)} %dynamic-slice_bitcast_fusion.4), channel_id=1, source_target_pairs={{0,2},{2,0},{4,6},{6,4},{8,10},{10,8},{12,14},{14,12},{1,3},{3,1},... | collective-permute-start | bytes 245768 | tf_op jit(solution)/shard_map/ppermute | solution.py:217
  58.4 5.6 %collective-permute-start.14 = (f32[160,128]{1,0:T(8,128)S(1)}, f32[160,128]{1,0:T(8,128)S(1)}, u32[]{:S(2)}, u32[]{:S(2)}) collective-permute-start(f32[160,128]{1,0:T(8,128)S(1)} %bitcast_add_fusion.2), channel_id=1, source_target_pairs={{0,2},{2,0},{4,6},{6,4},{8,10},{10,8},{12,14},{14,12},{1,3},{3,1},... | collective-permute-start | bytes 245768 | tf_op jit(solution)/shard_map/ppermute | solution.py:229
  60.1 8.3 %collective-permute-start.3 = (f32[160,128]{1,0:T(8,128)S(1)}, f32[160,128]{1,0:T(8,128)S(1)}, u32[]{:S(2)}, u32[]{:S(2)}) collective-permute-start(f32[160,128]{1,0:T(8,128)S(1)} %get-tuple-element.18), channel_id=1, source_target_pairs={{0,4},{2,6},{4,8},{6,10},{8,12},{10,14},{12,0},{14,2},{1,5},{3,7},... | collective-permute-start | bytes 245768 | tf_op jit(solution)/shard_map/ppermute | solution.py:217
  60.2 9.8 %collective-permute-start.5 = (f32[160,128]{1,0:T(8,128)S(1)}, f32[160,128]{1,0:T(8,128)S(1)}, u32[]{:S(2)}, u32[]{:S(2)}) collective-permute-start(f32[160,128]{1,0:T(8,128)S(1)} %get-tuple-element.19), channel_id=1, source_target_pairs={{0,12},{2,14},{4,0},{6,2},{8,4},{10,6},{12,8},{14,10},{1,13},{3,15... | collective-permute-start | bytes 245768 | tf_op jit(solution)/shard_map/ppermute | solution.py:217
  64.0 21.7 %collective-permute-start.4 = (f32[160,128]{1,0:T(8,128)S(1)}, f32[160,128]{1,0:T(8,128)S(1)}, u32[]{:S(2)}, u32[]{:S(2)}) collective-permute-start(f32[160,128]{1,0:T(8,128)S(1)} %get-tuple-element.20), channel_id=1, source_target_pairs={{0,8},{2,10},{4,12},{6,14},{8,0},{10,2},{12,4},{14,6},{1,9},{3,11}... | collective-permute-start | bytes 245768 | tf_op jit(solution)/shard_map/ppermute | solution.py:217
  64.0 38.8 %collective-permute-start.17 = (f32[320,128]{1,0:T(8,128)S(1)}, f32[320,128]{1,0:T(8,128)S(1)}, u32[]{:S(2)}, u32[]{:S(2)}) collective-permute-start(f32[320,128]{1,0:T(8,128)S(1)} %get-tuple-element.12), channel_id=1, source_target_pairs={{0,4},{2,6},{4,8},{6,10},{8,12},{10,14},{12,0},{14,2},{1,5},{3,7},... | collective-permute-start | bytes 491528 | tf_op jit(solution)/shard_map/ppermute | solution.py:229
  64.6 38.1 %collective-permute-start.16 = (f32[320,128]{1,0:T(8,128)S(1)}, f32[320,128]{1,0:T(8,128)S(1)}, u32[]{:S(2)}, u32[]{:S(2)}) collective-permute-start(f32[320,128]{1,0:T(8,128)S(1)} %get-tuple-element.12), channel_id=1, source_target_pairs={{0,8},{2,10},{4,12},{6,14},{8,0},{10,2},{12,4},{14,6},{1,9},{3,11}... | collective-permute-start | bytes 491528 | tf_op jit(solution)/shard_map/ppermute | solution.py:229
  68.4 24.7 %collective-permute-start.15 = (f32[320,128]{1,0:T(8,128)S(1)}, f32[320,128]{1,0:T(8,128)S(1)}, u32[]{:S(2)}, u32[]{:S(2)}) collective-permute-start(f32[320,128]{1,0:T(8,128)S(1)} %get-tuple-element.12), channel_id=1, source_target_pairs={{0,12},{2,14},{4,0},{6,2},{8,4},{10,6},{12,8},{14,10},{1,13},{3,15... | collective-permute-start | bytes 491528 | tf_op jit(solution)/shard_map/ppermute | solution.py:229
  85.7 35.2 %collective-permute-start.8 = (f32[160,128]{1,0:T(8,128)S(1)}, f32[160,128]{1,0:T(8,128)S(1)}, u32[]{:S(2)}, u32[]{:S(2)}) collective-permute-start(f32[160,128]{1,0:T(8,128)S(1)} %get-tuple-element.14), channel_id=1, source_target_pairs={{0,4},{2,6},{4,8},{6,10},{8,12},{10,14},{12,0},{14,2},{1,5},{3,7},... | collective-permute-start | bytes 245768 | tf_op jit(solution)/shard_map/ppermute | solution.py:229
  85.7 35.1 %collective-permute-start.7 = (f32[160,128]{1,0:T(8,128)S(1)}, f32[160,128]{1,0:T(8,128)S(1)}, u32[]{:S(2)}, u32[]{:S(2)}) collective-permute-start(f32[160,128]{1,0:T(8,128)S(1)} %get-tuple-element.14), channel_id=1, source_target_pairs={{0,8},{2,10},{4,12},{6,14},{8,0},{10,2},{12,4},{14,6},{1,9},{3,11}... | collective-permute-start | bytes 245768 | tf_op jit(solution)/shard_map/ppermute | solution.py:229
  93.1 27.7 %collective-permute-start.6 = (f32[160,128]{1,0:T(8,128)S(1)}, f32[160,128]{1,0:T(8,128)S(1)}, u32[]{:S(2)}, u32[]{:S(2)}) collective-permute-start(f32[160,128]{1,0:T(8,128)S(1)} %get-tuple-element.14), channel_id=1, source_target_pairs={{0,12},{2,14},{4,0},{6,2},{8,4},{10,6},{12,8},{14,10},{1,13},{3,15... | collective-permute-start | bytes 245768 | tf_op jit(solution)/shard_map/ppermute | solution.py:229
  121.0 8.1 %collective-permute-start.9 = (f32[640,128]{1,0:T(8,128)S(1)}, f32[640,128]{1,0:T(8,128)S(1)}, u32[]{:S(2)}, u32[]{:S(2)}) collective-permute-start(f32[640,128]{1,0:T(8,128)S(1)} %constant_dynamic-slice_fusion.1), channel_id=1, source_target_pairs={{0,2},{2,0},{4,6},{6,4},{8,10},{10,8},{12,14},{14,12},{1,3},{3,1},... | collective-permute-start | bytes 983048 | tf_op jit(solution)/shard_map/ppermute | solution.py:229
  121.1 8.2 %copy-start.3 = (s32[2048]{0:T(1024)S(1)}, s32[2048]{0:T(1024)}, u32[]{:S(2)}) copy-start(s32[2048]{0:T(1024)} %param.7) | copy-start | bytes 24580
  121.1 8.2 %copy-start.4 = (f32[8]{0:T(128)S(1)}, f32[8]{0:T(128)}, u32[]{:S(2)}) copy-start(f32[8]{0:T(128)} %constant.148.clone) | copy-start | bytes 100
  121.2 10.2 %copy-start.1 = (f32[1280,128]{1,0:T(8,128)}, f32[1280,128]{1,0:T(8,128)S(1)}, u32[]{:S(2)}) copy-start(f32[1280,128]{1,0:T(8,128)S(1)} %constant_dynamic-slice_fusion.refs_1_) | copy-start | bytes 1966084
  121.2 9.6 %collective-permute-start.19 = (f32[1280,128]{1,0:T(8,128)S(1)}, f32[1280,128]{1,0:T(8,128)S(1)}, u32[]{:S(2)}, u32[]{:S(2)}) collective-permute-start(f32[1280,128]{1,0:T(8,128)S(1)} %constant_dynamic-slice_fusion.refs_1_), channel_id=1, source_target_pairs={{0,1},{1,0},{2,3},{3,2},{4,5},{5,4},{6,7},{7,6},{8,9},{9,8},{10,11... | collective-permute-start | bytes 1966088 | tf_op jit(solution)/shard_map/ppermute | solution.py:279
  129.2 2.2 %copy-start.2 = (f32[1280,128]{1,0:T(8,128)}, f32[1280,128]{1,0:T(8,128)S(1)}, u32[]{:S(2)}) copy-start(f32[1280,128]{1,0:T(8,128)S(1)} %maximum_select_fusion.refs_0_) | copy-start | bytes 1966084
  129.2 2.2 %collective-permute-start.18 = (f32[1280,128]{1,0:T(8,128)S(1)}, f32[1280,128]{1,0:T(8,128)S(1)}, u32[]{:S(2)}, u32[]{:S(2)}) collective-permute-start(f32[1280,128]{1,0:T(8,128)S(1)} %maximum_select_fusion.refs_0_), channel_id=1, source_target_pairs={{0,1},{1,0},{2,3},{3,2},{4,5},{5,4},{6,7},{7,6},{8,9},{9,8},{10,11... | collective-permute-start | bytes 1966088 | tf_op jit(solution)/shard_map/ppermute | solution.py:279
  130.8 0.8 copy-start.6
  131.6 0.8 copy-start.7
Sparse Core Ops, SparseCore 0:
  9.4 115.4 all-gather.1
